TPU v7x, 32 devices: a whole 2x2x4 slice. The times are simulated.
32 devices in a mesh: dp: 8 (over z, x), expert: 4 (over y, core).
Axes of the slice: x: 2, y: 2, z: 4, core: 2. Of those that a mesh axis runs over, the one named last changes fastest.
Arguments:
- step_inputs: bfloat16 [4096, 2048], P(('dp', 'expert')), may hold values from -6 to 6
- step_cotangent: bfloat16 [4096, 2048], P(('dp', 'expert')), may hold values from -6 to 6
- step_routes: int32 [4096, 1], P(('dp', 'expert')), may hold values from 0 to 3; in each aligned block of 128 rows (0 to 127, 128 to 255, ...) at most 40 rows name the same one
- step_gates: float32 [4096, 1], P(('dp', 'expert')), may hold values from 0.1 to 1
- next_inputs: bfloat16 [4096, 2048], P(('dp', 'expert')), may hold values from -6 to 6
- next_routes: int32 [4096, 1], P(('dp', 'expert')), may hold values from 0 to 3; in each aligned block of 128 rows (0 to 127, 128 to 255, ...) at most 40 rows name the same one
- next_gates: float32 [4096, 1], P(('dp', 'expert')), may hold values from 0.1 to 1
- master_weights: float32 [4, 2048, 3456], P('expert', 'dp'), may hold values from -4 to 4
- first_moment: float32 [4, 2048, 3456], P('expert', 'dp'), may hold values from -0.6 to 0.6
- second_moment: float32 [4, 2048, 3456], P('expert', 'dp'), may hold values from 0.01 to 0.2
- owner_plan: int32 [4], replicated, may hold values from 0 to 3, as said below
Outputs:
- layer_output: bfloat16 [4096, 2048], P(('dp', 'expert'))
- moved_weights: float32 [4, 2048, 3456], P('expert', 'dp')
- moved_first: float32 [4, 2048, 3456], P('expert', 'dp')
- moved_second: float32 [4, 2048, 3456], P('expert', 'dp')
Inputs may be any that keep to these rules, and one draw needn't show every extreme that they name: `step_routes`: among the 128 tokens of one device no expert is named more than 40 times. `next_routes`: among the 128 tokens of one device no expert is named more than 40 times. `owner_plan`: every index appears once.
All inputs are finite; a program needn't handle non-finite values.
Results may differ from a plain program's by a relative error of at most 0.025.
Values may be sent and summed in bfloat16 or wider, within the bound.
A program may use at most 128 MiB of HBM per device.

v0:
```python
import jax
import jax.numpy as jnp
from jax import lax
from jax.sharding import PartitionSpec as P

D = 2048
HID = 1152
EXPERTS = 4
CAP = 40


beta_one = 0.9
beta_two = 0.95
learn_rate = 0.2
decay_rate = 0.1
adam_step = 10.0
adam_eps = 1e-08


def slot_targets(routes, capacity):
    pair_ids = routes.reshape(-1)
    one_hot = (pair_ids[:, None] == jnp.arange(EXPERTS, dtype=jnp.int32)[None, :]).astype(jnp.int32)
    earlier = jnp.cumsum(one_hot, axis=0) - one_hot
    slot_ids = jnp.sum(earlier * one_hot, axis=1)
    return pair_ids * capacity + slot_ids


def dispatch_pairs(targets, payload, capacity):
    selector = (
        lax.broadcasted_iota(jnp.int32, (EXPERTS * capacity, targets.shape[0]), 0)
        == targets[None, :]
    ).astype(jnp.bfloat16)
    filled = jnp.dot(selector, payload, preferred_element_type=jnp.float32).astype(jnp.bfloat16)
    return filled.reshape(EXPERTS, capacity, payload.shape[1])


def shards(
    step_inputs,
    step_cotangent,
    step_routes,
    step_gates,
    next_inputs,
    next_routes,
    next_gates,
    master_weights,
    first_moment,
    second_moment,
    owner_plan,
):
    groups = lax.axis_size("expert")
    split = groups // EXPERTS
    width = master_weights.shape[2] // 3
    in_scale = D ** (-0.5)
    out_scale = HID ** (-0.5)
    topk_count = step_routes.shape[1]
    step_targets = slot_targets(step_routes, CAP)
    input_pairs = jnp.repeat(step_inputs, topk_count, axis=0)
    scaled_pairs = (
        jnp.repeat(step_cotangent, topk_count, axis=0).astype(jnp.float32) * step_gates
    ).astype(jnp.bfloat16)
    send_inputs = jnp.repeat(dispatch_pairs(step_targets, input_pairs, CAP), split, axis=0)
    send_scaled = jnp.repeat(dispatch_pairs(step_targets, scaled_pairs, CAP), split, axis=0)
    got_inputs, got_scaled = (
        lax.all_to_all(send_inputs, "expert", split_axis=0, concat_axis=0, tiled=True),
        lax.all_to_all(send_scaled, "expert", split_axis=0, concat_axis=0, tiled=True),
    )
    flat_inputs = got_inputs.reshape(-1, D)
    flat_scaled = got_scaled.reshape(-1, D)
    old_weights = master_weights[0]
    piece = lax.all_gather(old_weights.astype(jnp.bfloat16), "dp", axis=0, tiled=True)
    inputs_part = flat_inputs
    scaled_part = flat_scaled
    gate_sum = jnp.dot(inputs_part, piece[:, :width], preferred_element_type=jnp.float32)
    up_sum = jnp.dot(inputs_part, piece[:, width : 2 * width], preferred_element_type=jnp.float32)
    down_sum = jnp.dot(scaled_part, piece[:, 2 * width :], preferred_element_type=jnp.float32)
    gate_sum, up_sum, down_sum = (gate_sum, up_sum, down_sum)
    gate_pre = gate_sum * in_scale
    up_pre = up_sum * in_scale
    down_back = down_sum * out_scale
    sigmoid_gate = jax.nn.sigmoid(gate_pre)
    silu_gate = gate_pre * sigmoid_gate
    activation = (silu_gate * up_pre).astype(jnp.bfloat16)
    gate_grad = (
        down_back * up_pre * sigmoid_gate * (1.0 + gate_pre * (1.0 - sigmoid_gate))
    ).astype(jnp.bfloat16)
    up_grad = (down_back * silu_gate).astype(jnp.bfloat16)
    inputs_part = flat_inputs
    scaled_part = flat_scaled
    contract = (((0,), (0,)), ((), ()))
    gate_part = (
        lax.dot_general(inputs_part, gate_grad, contract, preferred_element_type=jnp.float32)
        * in_scale
    )
    up_part = (
        lax.dot_general(inputs_part, up_grad, contract, preferred_element_type=jnp.float32)
        * in_scale
    )
    down_part = (
        lax.dot_general(scaled_part, activation, contract, preferred_element_type=jnp.float32)
        * out_scale
    )
    gradient = lax.psum_scatter(
        jnp.concatenate([gate_part, up_part, down_part], axis=1).astype(jnp.bfloat16),
        "dp",
        scatter_dimension=0,
        tiled=True,
    ).astype(jnp.float32)
    first_new = beta_one * first_moment[0] + (1.0 - beta_one) * gradient
    second_new = beta_two * second_moment[0] + (1.0 - beta_two) * gradient * gradient
    first_hat = first_new / (1.0 - beta_one**adam_step)
    second_hat = second_new / (1.0 - beta_two**adam_step)
    new_weights = old_weights - learn_rate * (
        first_hat / (jnp.sqrt(second_hat) + adam_eps) + decay_rate * old_weights
    )
    positions = jnp.arange(groups, dtype=jnp.int32)
    holder = jnp.sum(
        jnp.where(owner_plan[:, None] == positions[None, :], positions[:, None], 0), axis=0
    )
    stacked = jnp.stack([new_weights, first_new, second_new])
    rows_here = stacked.shape[1]
    pieces = stacked.reshape(3, groups, rows_here // groups, stacked.shape[2])
    spread = lax.all_to_all(
        pieces.astype(jnp.bfloat16), "expert", split_axis=1, concat_axis=1, tiled=True
    ).astype(pieces.dtype)
    ordered = jnp.take(spread, holder, axis=1)
    collected = lax.all_to_all(
        ordered.astype(jnp.bfloat16), "expert", split_axis=1, concat_axis=1, tiled=True
    ).astype(ordered.dtype)
    relocated = collected.reshape(3, rows_here, stacked.shape[2])
    serve_expert = positions // split
    serve_full = lax.all_gather(new_weights.astype(jnp.bfloat16), "dp", axis=0, tiled=True)
    next_targets = slot_targets(next_routes, CAP)
    next_pairs = jnp.repeat(next_inputs, topk_count, axis=0)
    send_next = jnp.take(dispatch_pairs(next_targets, next_pairs, CAP), serve_expert, axis=0)
    received = lax.all_to_all(send_next, "expert", split_axis=0, concat_axis=0, tiled=True)
    flat_rows = received.reshape(-1, D)
    gate_next = (
        jnp.dot(flat_rows, serve_full[:, :width], preferred_element_type=jnp.float32) * in_scale
    )
    up_next = (
        jnp.dot(flat_rows, serve_full[:, width : 2 * width], preferred_element_type=jnp.float32)
        * in_scale
    )
    next_activation = (gate_next * jax.nn.sigmoid(gate_next) * up_next).astype(jnp.bfloat16)
    slab_partial = (
        lax.dot_general(
            next_activation,
            serve_full[:, 2 * width :],
            (((1,), (1,)), ((), ())),
            preferred_element_type=jnp.float32,
        )
        * out_scale
    )
    partials = slab_partial.astype(jnp.bfloat16).reshape(received.shape[0], received.shape[1], D)
    returned = lax.all_to_all(partials, "expert", split_axis=0, concat_axis=0, tiled=True)
    selector = (serve_expert[None, :] == jnp.arange(EXPERTS, dtype=jnp.int32)[:, None]).astype(
        jnp.bfloat16
    )
    expert_sums = jnp.dot(
        selector, returned.reshape(groups, -1), preferred_element_type=jnp.float32
    ).reshape(EXPERTS * CAP, D)
    pair_sums = jnp.take(expert_sums, next_targets, axis=0)
    weighted = pair_sums * next_gates
    layer_output = jnp.sum(weighted.reshape(-1, topk_count, D), axis=1).astype(jnp.bfloat16)
    return (layer_output, relocated[0][None], relocated[1][None], relocated[2][None])


def solution(mesh):
    placed = (
        P(("dp", "expert"), None),
        P(("dp", "expert"), None),
        P(("dp", "expert"), None),
        P(("dp", "expert"), None),
        P(("dp", "expert"), None),
        P(("dp", "expert"), None),
        P(("dp", "expert"), None),
        P("expert", "dp", None),
        P("expert", "dp", None),
        P("expert", "dp", None),
        P(),
    )
    return jax.shard_map(
        shards,
        mesh=mesh,
        in_specs=placed,
        out_specs=(
            P(("dp", "expert"), None),
            P("expert", "dp", None),
            P("expert", "dp", None),
            P("expert", "dp", None),
        ),
        check_vma=False,
    )
```

profile of v0, /device:TPU:0, one launch (start us, length us, event | category | flops | bytes accessed | tf_op | source)
XLA Modules:
  0.0 720.2 jit_solution(4335262609261996267)
XLA Ops:
  7.2 5.2 copy.30
  12.4 3.4 bitcast_convert_fusion
  17.6 4.2 all-to-all-start.1
  23.0 9.0 %all-to-all-done.1 = bf16[4,40,2048]{2,1,0:T(8,128)(2,1)S(1)} async-done(((bf16[4,40,2048]{2,1,0:T(8,128)(2,1)}), bf16[4,40,2048]{2,1,0:T(8,128)(2,1)S(1)}, u32[]{:S(2)}, u32[]{:S(2)}) %all-to-all-start.1) | async-done | bytes 655392 | tf_op jit(solution)/shard_map/all_to_all | solution.py:64
  32.0 3.5 all-to-all-start.2
  35.6 178.9 %all-gather.3.cloned.1.call-done = bf16[2048,3456]{0,1:T(8,128)(2,1)} async-done(((bf16[256,3456]{0,1:T(8,128)(2,1)}), bf16[2048,3456]{0,1:T(8,128)(2,1)}) %all-gather.3.cloned.1.call-update) | async-done | bytes 14155792 | tf_op jit(solution)/shard_map/all_gather | solution.py:70
  214.5 4.0 fusion.27
  218.5 4.0 fusion.21
  222.6 1.5 fusion.1
  224.1 4.0 fusion.24
  229.6 1.5 fusion.2
  231.2 22.7 %pad_maximum_fusion = bf16[2048,3456]{0,1:T(8,128)(2,1)} fusion(bf16[2048,1152]{0,1:T(8,128)(2,1)S(1)} %fusion.2, bf16[2048,1152]{0,1:T(8,128)(2,1)S(1)} %fusion.1, bf16[2048,1152]{0,1:T(8,128)(2,1)S(1)} %fusion), kind=kLoop, calls=%fused_computation.3 | loop fusion | flops 42467328 | bytes 28311552 | tf_op jit(solution)/shard_map/concatenate | solution.py:103
  254.2 5.2 copy.31
  259.3 5.6 copy.32
  264.9 217.0 %reduce-scatter.2.cloned.1.call-done = bf16[256,3456]{0,1:T(8,128)(2,1)} async-done(((bf16[2048,3456]{0,1:T(8,128)(2,1)}), bf16[256,3456]{0,1:T(8,128)(2,1)}) %reduce-scatter.2.cloned.1.call-update) | async-done | bytes 1769488 | tf_op jit(solution)/shard_map/reduce_scatter | solution.py:102
  481.8 7.5 %fusion.48 = (bf16[256,3456]{0,1:T(8,128)(2,1)}, bf16[256,3456]{0,1:T(8,128)(2,1)}, bf16[256,3456]{0,1:T(8,128)(2,1)S(1)}) fusion(bf16[256,3456]{0,1:T(8,128)(2,1)} %reduce-scatter.2.cloned.1.call-done, f32[1,256,3456]{1,2,0:T(8,128)} %copy.31, f32[1,256,3456]{1,2,0:T(8,128)} %copy.32, f32[1,256,3456]{1,2,0:T(8,128)} %copy.30), kind=kLoop, calls=%fused_computation.47 | loop fusion | flops 16809984 | bytes 17694720 | tf_op jit(solution)/shard_map/convert.4
  489.4 3.8 copy.33
  493.2 3.9 copy.34
  497.1 2.2 copy.35
  499.3 6.0 pad_maximum_fusion.1
  505.4 5.2 all-to-all-start.4
  513.1 57.7 %all-to-all-done.4 = bf16[3,4,64,3456]{3,2,0,1:T(8,128)(2,1)} async-done(((bf16[3,4,64,3456]{3,2,0,1:T(8,128)(2,1)}), bf16[3,4,64,3456]{3,2,0,1:T(8,128)(2,1)}, u32[]{:S(2)}, u32[]{:S(2)}) %all-to-all-start.4) | async-done | bytes 5308448 | tf_op jit(solution)/shard_map/all_to_all | solution.py:122
  570.7 3.5 all-to-all-start
  574.2 6.0 gather_fusion.2
  580.2 6.0 fusion.3
  586.2 5.1 all-to-all-start.5
  591.3 93.1 %all-gather.5.cloned.1.call-done = bf16[2048,3456]{0,1:T(8,128)(2,1)} async-done(((bf16[256,3456]{0,1:T(8,128)(2,1)}), bf16[2048,3456]{0,1:T(8,128)(2,1)}) %all-gather.5.cloned.1.call-update) | async-done | bytes 14155792 | tf_op jit(solution)/shard_map/all_gather | solution.py:131
  684.4 4.0 fusion.30
  688.4 7.6 %fusion.42 = bf16[160,2048]{1,0:T(8,128)(2,1)} fusion(bf16[2048,3456]{0,1:T(8,128)(2,1)} %all-gather.5.cloned.1.call-done, bf16[160,2048]{1,0:T(8,128)(2,1)S(1)} %bitcast.90, f32[160,1152]{1,0:T(8,128)S(1)} %fusion.30), kind=kOutput, calls=%fused_computation.42 | convolution fusion | flops 1511895040 | bytes 11485184 | tf_op jit(solution)/shard_map/dot_general | solution.py:146
  696.0 3.7 all-to-all-start.3
  699.8 6.9 fusion.76
  706.7 3.1 all-to-all-done.3
  (55 shorter events, 11.1 us)
Async XLA Ops:
  7.2 9.2 %copy-start = (bf16[128,2048]{1,0:T(8,128)(2,1)S(1)}, bf16[128,2048]{1,0:T(8,128)(2,1)}, u32[]{:S(2)}) copy-start(bf16[128,2048]{1,0:T(8,128)(2,1)} %param.11) | copy-start | bytes 1572868
  7.2 207.3 %all-gather.3.cloned.1.call-start = ((), (), s32[]{:S(2)}) async-start(), calls=%async_computation.7 | async-start | bytes 15925248 | tf_op jit(solution)/shard_map/all_gather | solution.py:70
  12.4 3.5 copy-start.5
  12.4 9.4 %copy-start.3 = (bf16[128,2048]{1,0:T(8,128)(2,1)S(1)}, bf16[128,2048]{1,0:T(8,128)(2,1)}, u32[]{:S(2)}) copy-start(bf16[128,2048]{1,0:T(8,128)(2,1)} %param.12) | copy-start | bytes 1572868
  12.4 9.4 %copy-start.6 = (f32[128,1]{0,1:T(1,128)S(1)}, f32[128,1]{0,1:T(1,128)}, u32[]{:S(2)}) copy-start(f32[128,1]{0,1:T(1,128)} %param.14) | copy-start | bytes 1540
  17.6 14.5 %all-to-all-start.1 = ((bf16[4,40,2048]{2,1,0:T(8,128)(2,1)}), bf16[4,40,2048]{2,1,0:T(8,128)(2,1)S(1)}, u32[]{:S(2)}, u32[]{:S(2)}) async-start(bf16[4,40,2048]{2,1,0:T(8,128)(2,1)} %bitcast.8), calls=%async_computation.1 | async-start | bytes 1310720 | tf_op jit(solution)/shard_map/all_to_all | solution.py:64
  32.0 186.5 %all-to-all-start.2 = ((bf16[4,40,2048]{2,1,0:T(8,128)(2,1)}), bf16[4,40,2048]{2,1,0:T(8,128)(2,1)S(1)}, u32[]{:S(2)}, u32[]{:S(2)}) async-start(bf16[4,40,2048]{2,1,0:T(8,128)(2,1)} %bitcast.11), calls=%async_computation.2 | async-start | bytes 1310720 | tf_op jit(solution)/shard_map/all_to_all | solution.py:65
  35.5 446.3 %reduce-scatter.2.cloned.1.call-start = ((), (), s32[]{:S(2)}) async-start(), calls=%async_computation.8 | async-start | bytes 15925248 | tf_op jit(solution)/shard_map/reduce_scatter | solution.py:102
  253.9 430.5 %all-gather.5.cloned.1.call-start = ((), (), s32[]{:S(2)}) async-start(), calls=%async_computation.9 | async-start | bytes 15925248 | tf_op jit(solution)/shard_map/all_gather | solution.py:131
  505.3 5.2 copy-start.4
  505.3 5.7 copy-start.2
  505.3 6.6 copy-start.8
  505.4 65.4 %all-to-all-start.4 = ((bf16[3,4,64,3456]{3,2,0,1:T(8,128)(2,1)}), bf16[3,4,64,3456]{3,2,0,1:T(8,128)(2,1)}, u32[]{:S(2)}, u32[]{:S(2)}) async-start(bf16[3,4,64,3456]{3,2,0,1:T(8,128)(2,1)} %pad_maximum_fusion.1), calls=%async_computation.5 | async-start | bytes 10616832 | tf_op jit(solution)/shard_map/all_to_all | solution.py:122
  570.7 15.5 %all-to-all-start = ((bf16[4,40,2048]{2,1,0:T(8,128)(2,1)}), bf16[4,40,2048]{2,1,0:T(8,128)(2,1)S(1)}, u32[]{:S(2)}, u32[]{:S(2)}) async-start(bf16[4,40,2048]{2,1,0:T(8,128)(2,1)} %broadcast_select_fusion), calls=%async_computation | async-start | bytes 1310720 | tf_op jit(solution)/shard_map/all_to_all | solution.py:135
  586.2 109.8 %all-to-all-start.5 = ((bf16[3,4,64,3456]{3,2,0,1:T(8,128)(2,1)}), bf16[3,4,64,3456]{3,2,0,1:T(8,128)(2,1)}, u32[]{:S(2)}, u32[]{:S(2)}) async-start(bf16[3,4,64,3456]{3,2,0,1:T(8,128)(2,1)} %fusion.3), calls=%async_computation.6 | async-start | bytes 10616832 | tf_op jit(solution)/shard_map/all_to_all | solution.py:126
  696.0 13.7 %all-to-all-start.3 = ((bf16[4,40,2048]{2,1,0:T(8,128)(2,1)}), bf16[4,40,2048]{2,1,0:T(8,128)(2,1)S(1)}, u32[]{:S(2)}, u32[]{:S(2)}) async-start(bf16[4,40,2048]{2,1,0:T(8,128)(2,1)} %bitcast.14), calls=%async_computation.4 | async-start | bytes 1310720 | tf_op jit(solution)/shard_map/all_to_all | solution.py:155
  710.8 2.9 copy-start.1
  711.7 1.0 copy-start.7
Sparse Core Ops, SparseCore 0:
  16.0 198.4 all-gather.2
  254.1 227.7 reduce-scatter.1
  489.5 194.8 all-gather.4
where the time goes:
time: 721 us; the launch traced here: 720 us
  waiting for transfers between devices  559 us (78%)
  other arithmetic  48.7 us (7%)
  local copies, waits for them, and re-layouts  41.7 us (6%)
  matrix products  31.5 us (4%)
  starting transfers between devices  25.5 us (4%)
  between operations  14 us (2%)
    reduce_scatter x1, waiting for transfers between devices, shards(): lax.psum_scatter(jnp.concatenate([gate_part, up_part, down_part], axis=1)...  217 us
    all_gather x1, waiting for transfers between devices, shards(): lax.all_gather(old_weights.astype(jnp.bfloat16), 'dp', axis=0, tiled=True)  179 us
    all_gather x1, waiting for transfers between devices, shards(): lax.all_gather(new_weights.astype(jnp.bfloat16), 'dp', axis=0, tiled=True)  93.1 us
    all_to_all x1, waiting for transfers between devices, shards(): lax.all_to_all(pieces.astype(jnp.bfloat16), 'expert', split_axis=1, conca...  57.7 us
    concatenate x1, other arithmetic, shards(): jnp.concatenate([gate_part, up_part, down_part], axis=1)  22.7 us
    unnamed x22, local copies, waits for them, and re-layouts  16.5 us
  transfers between devices with their start and end apart: 9, of which 6 were waited for; matrix products, arithmetic and copies ran while one was open for 9% of the time, Pallas kernels for 0%

commit v1 on v0

v1 whole, which is shorter than its diff:
```python
import jax
import jax.numpy as jnp
from jax import lax
from jax.sharding import PartitionSpec as P

D = 2048
HID = 1152
EXPERTS = 4
CAP = 40


beta_one = 0.9
beta_two = 0.95
learn_rate = 0.2
decay_rate = 0.1
adam_step = 10.0
adam_eps = 1e-08


def slot_targets(routes, capacity):
    pair_ids = routes.reshape(-1)
    count = pair_ids.shape[0]
    before = lax.broadcasted_iota(jnp.int32, (count, count), 1) < lax.broadcasted_iota(
        jnp.int32, (count, count), 0
    )
    same = pair_ids[:, None] == pair_ids[None, :]
    slot_ids = jnp.sum(jnp.where(before & same, 1, 0), axis=1, dtype=jnp.int32)
    return pair_ids * capacity + slot_ids


def exchange(array, axis):
    return lax.all_to_all(array, axis, split_axis=0, concat_axis=0, tiled=True)


def hidden_terms(gate_pre, up_pre, down_back):
    sigmoid_gate = jax.nn.sigmoid(gate_pre)
    silu_gate = gate_pre * sigmoid_gate
    activation = (silu_gate * up_pre).astype(jnp.bfloat16)
    gate_grad = (
        down_back * up_pre * sigmoid_gate * (1.0 + gate_pre * (1.0 - sigmoid_gate))
    ).astype(jnp.bfloat16)
    up_grad = (down_back * silu_gate).astype(jnp.bfloat16)
    return activation, gate_grad, up_grad


def gradient_by_weights(flat_inputs, flat_scaled, old_weights, width, in_scale, out_scale):
    piece = lax.all_gather(old_weights.astype(jnp.bfloat16), "dp", axis=0, tiled=True)
    gate_pre = jnp.dot(flat_inputs, piece[:, :width], preferred_element_type=jnp.float32) * in_scale
    up_pre = (
        jnp.dot(flat_inputs, piece[:, width : 2 * width], preferred_element_type=jnp.float32)
        * in_scale
    )
    down_back = (
        jnp.dot(flat_scaled, piece[:, 2 * width :], preferred_element_type=jnp.float32) * out_scale
    )
    activation, gate_grad, up_grad = hidden_terms(gate_pre, up_pre, down_back)
    contract = (((0,), (0,)), ((), ()))
    parts = [
        lax.dot_general(rows, terms, contract, preferred_element_type=jnp.float32) * scale
        for rows, terms, scale in (
            (flat_inputs, gate_grad, in_scale),
            (flat_inputs, up_grad, in_scale),
            (flat_scaled, activation, out_scale),
        )
    ]
    return lax.psum_scatter(
        jnp.concatenate(parts, axis=1).astype(jnp.bfloat16),
        "dp",
        scatter_dimension=0,
        tiled=True,
    ).astype(jnp.float32)


def gradient_by_tokens(flat_inputs, flat_scaled, old_weights, width, in_scale, out_scale):
    shards_dp = lax.axis_size("dp")
    depth = old_weights.shape[0]
    columns = width // shards_dp
    all_inputs = lax.all_gather(flat_inputs, "dp", axis=0, tiled=True)
    all_scaled = lax.all_gather(flat_scaled, "dp", axis=0, tiled=True)
    turned = old_weights.astype(jnp.bfloat16).T.reshape(3, shards_dp, columns, depth)
    mine = exchange(turned.transpose(1, 0, 2, 3), "dp")
    mine = mine.transpose(1, 2, 0, 3).reshape(3 * columns, shards_dp * depth)
    contract = (((1,), (1,)), ((), ()))
    gate_up = (
        lax.dot_general(
            mine[: 2 * columns], all_inputs, contract, preferred_element_type=jnp.float32
        )
        * in_scale
    )
    down_back = (
        lax.dot_general(
            mine[2 * columns :], all_scaled, contract, preferred_element_type=jnp.float32
        )
        * out_scale
    )
    activation, gate_grad, up_grad = hidden_terms(gate_up[:columns], gate_up[columns:], down_back)
    gate_up_part = (
        jnp.dot(
            jnp.concatenate([gate_grad, up_grad], axis=0),
            all_inputs,
            preferred_element_type=jnp.float32,
        )
        * in_scale
    )
    down_part = jnp.dot(activation, all_scaled, preferred_element_type=jnp.float32) * out_scale
    grads = jnp.concatenate([gate_up_part.astype(jnp.bfloat16), down_part.astype(jnp.bfloat16)], axis=0)
    grads = grads.reshape(3, columns, shards_dp, depth).transpose(2, 0, 1, 3)
    back = exchange(grads, "dp").transpose(1, 0, 2, 3).reshape(3 * width, depth)
    return back.T.astype(jnp.float32)


def forward_by_weights(flat_rows, new_weights, width, in_scale, out_scale):
    full = lax.all_gather(new_weights, "dp", axis=0, tiled=True)
    gate = jnp.dot(flat_rows, full[:, :width], preferred_element_type=jnp.float32) * in_scale
    up = (
        jnp.dot(flat_rows, full[:, width : 2 * width], preferred_element_type=jnp.float32)
        * in_scale
    )
    activation = (gate * jax.nn.sigmoid(gate) * up).astype(jnp.bfloat16)
    return (
        lax.dot_general(
            activation,
            full[:, 2 * width :],
            (((1,), (1,)), ((), ())),
            preferred_element_type=jnp.float32,
        )
        * out_scale
    ).astype(jnp.bfloat16)


def forward_by_tokens(flat_rows, new_weights, width, in_scale, out_scale):
    shards_dp = lax.axis_size("dp")
    depth = new_weights.shape[0]
    count = flat_rows.shape[0]
    slices = exchange(flat_rows.reshape(count, shards_dp, depth).transpose(1, 0, 2), "dp")
    slices = slices.reshape(shards_dp * count, depth)
    partial_pre = (
        jnp.dot(slices, new_weights[:, : 2 * width], preferred_element_type=jnp.float32) * in_scale
    ).astype(jnp.bfloat16)
    pre = lax.psum_scatter(partial_pre, "dp", scatter_dimension=0, tiled=True).astype(jnp.float32)
    gate, up = pre[:, :width], pre[:, width:]
    activation = (gate * jax.nn.sigmoid(gate) * up).astype(jnp.bfloat16)
    gathered = lax.all_gather(activation, "dp", axis=0, tiled=True)
    out = (
        lax.dot_general(
            gathered,
            new_weights[:, 2 * width :],
            (((1,), (1,)), ((), ())),
            preferred_element_type=jnp.float32,
        )
        * out_scale
    ).astype(jnp.bfloat16)
    back = exchange(out.reshape(shards_dp, count, depth), "dp")
    return back.transpose(1, 0, 2).reshape(count, shards_dp * depth)


def dispatch_pairs(targets, payload, capacity):
    selector = (
        lax.broadcasted_iota(jnp.int32, (EXPERTS * capacity, targets.shape[0]), 0)
        == targets[None, :]
    ).astype(jnp.bfloat16)
    filled = jnp.dot(selector, payload, preferred_element_type=jnp.float32).astype(jnp.bfloat16)
    return filled.reshape(EXPERTS, capacity, payload.shape[1])


def shards(
    step_inputs,
    step_cotangent,
    step_routes,
    step_gates,
    next_inputs,
    next_routes,
    next_gates,
    master_weights,
    first_moment,
    second_moment,
    owner_plan,
):
    groups = lax.axis_size("expert")
    split = groups // EXPERTS
    width = master_weights.shape[2] // 3
    in_scale = D ** (-0.5)
    out_scale = HID ** (-0.5)
    topk_count = step_routes.shape[1]
    step_targets = slot_targets(step_routes, CAP)
    input_pairs = jnp.repeat(step_inputs, topk_count, axis=0)
    scaled_pairs = (
        jnp.repeat(step_cotangent, topk_count, axis=0).astype(jnp.float32) * step_gates
    ).astype(jnp.bfloat16)
    send_inputs = jnp.repeat(dispatch_pairs(step_targets, input_pairs, CAP), split, axis=0)
    send_scaled = jnp.repeat(dispatch_pairs(step_targets, scaled_pairs, CAP), split, axis=0)
    flat_inputs = exchange(send_inputs, "expert").reshape(-1, D)
    flat_scaled = exchange(send_scaled, "expert").reshape(-1, D)
    old_weights = master_weights[0]
    shards_dp = lax.axis_size("dp")
    by_tokens = 2 * shards_dp * flat_inputs.shape[0] <= 3 * width and width % shards_dp == 0
    gradient = (gradient_by_tokens if by_tokens else gradient_by_weights)(
        flat_inputs, flat_scaled, old_weights, width, in_scale, out_scale
    )
    first_new = beta_one * first_moment[0] + (1.0 - beta_one) * gradient
    second_new = beta_two * second_moment[0] + (1.0 - beta_two) * gradient * gradient
    first_hat = first_new / (1.0 - beta_one**adam_step)
    second_hat = second_new / (1.0 - beta_two**adam_step)
    new_weights = old_weights - learn_rate * (
        first_hat / (jnp.sqrt(second_hat) + adam_eps) + decay_rate * old_weights
    )
    positions = jnp.arange(groups, dtype=jnp.int32)
    holder = jnp.sum(
        jnp.where(owner_plan[:, None] == positions[None, :], positions[:, None], 0), axis=0
    )
    stacked = jnp.stack([new_weights, first_new, second_new])
    rows_here = stacked.shape[1]
    pieces = stacked.reshape(3, groups, rows_here // groups, stacked.shape[2])
    spread = lax.all_to_all(
        pieces.astype(jnp.bfloat16), "expert", split_axis=1, concat_axis=1, tiled=True
    ).astype(pieces.dtype)
    ordered = jnp.concatenate(
        [lax.dynamic_slice_in_dim(spread, holder[p], 1, axis=1) for p in range(groups)], axis=1
    )
    collected = lax.all_to_all(
        ordered.astype(jnp.bfloat16), "expert", split_axis=1, concat_axis=1, tiled=True
    ).astype(ordered.dtype)
    relocated = collected.reshape(3, rows_here, stacked.shape[2])
    next_targets = slot_targets(next_routes, CAP)
    next_pairs = jnp.repeat(next_inputs, topk_count, axis=0)
    send_next = jnp.repeat(dispatch_pairs(next_targets, next_pairs, CAP), split, axis=0)
    received = exchange(send_next, "expert")
    flat_rows = received.reshape(-1, D)
    partials = (forward_by_tokens if by_tokens else forward_by_weights)(
        flat_rows, new_weights.astype(jnp.bfloat16), width, in_scale, out_scale
    )
    returned = exchange(partials.reshape(received.shape), "expert").reshape(-1, D)
    places = lax.broadcasted_iota(jnp.int32, (next_targets.shape[0], groups * CAP), 1)
    selector = (
        next_targets[:, None] == (places // (split * CAP)) * CAP + places % CAP
    ).astype(jnp.bfloat16)
    pair_sums = jnp.dot(selector, returned, preferred_element_type=jnp.float32)
    weighted = pair_sums * next_gates
    layer_output = jnp.sum(weighted.reshape(-1, topk_count, D), axis=1).astype(jnp.bfloat16)
    return (layer_output, relocated[0][None], relocated[1][None], relocated[2][None])


def solution(mesh):
    placed = (
        P(("dp", "expert"), None),
        P(("dp", "expert"), None),
        P(("dp", "expert"), None),
        P(("dp", "expert"), None),
        P(("dp", "expert"), None),
        P(("dp", "expert"), None),
        P(("dp", "expert"), None),
        P("expert", "dp", None),
        P("expert", "dp", None),
        P("expert", "dp", None),
        P(),
    )
    return jax.shard_map(
        shards,
        mesh=mesh,
        in_specs=placed,
        out_specs=(
            P(("dp", "expert"), None),
            P("expert", "dp", None),
            P("expert", "dp", None),
            P("expert", "dp", None),
        ),
        check_vma=False,
    )
```

time: 721 us -> 612 us (0.85)
  waiting for transfers between devices: 559 us -> 428 us
  other arithmetic: 48.7 us -> 19.1 us
  blocking collectives: 0 us -> 27.8 us
  starting transfers between devices: 25.5 us -> 37.5 us
  between operations: 14 us -> 21.5 us
    all_gather x2 -> x3, waiting for transfers between devices: 272 us -> 121 us  [the longest x1 81.7 us: gradient_by_tokens(): all_scaled = lax.all_gather(flat_scaled, 'dp', axis=0, tiled=True)]
    all_to_all x4 -> x6, waiting for transfers between devices: 12.1 us -> 120 us  [exchange(): return lax.all_to_all(array, axis, split_axis=0, concat_axis=0, tiled=True)]
    reduce_scatter x1, waiting for transfers between devices: 217 us -> 111 us  [forward_by_tokens(): lax.psum_scatter(partial_pre, 'dp', scatter_dimension=0, tiled=True)]
    all_to_all x1, waiting for transfers between devices: 0.01 us -> 58.6 us  [shards(): lax.all_to_all(ordered.astype(jnp.bfloat16), 'expert', split_axis=1, conc...]
    all_to_all x1, waiting for transfers between devices: 57.7 us -> 17.7 us  [shards(): lax.all_to_all(pieces.astype(jnp.bfloat16), 'expert', split_axis=1, conca...]
    all_to_all x0 -> x2, blocking collectives: none -> 27.8 us  [exchange(): return lax.all_to_all(array, axis, split_axis=0, concat_axis=0, tiled=True)]
    concatenate x1 -> x2, other arithmetic: 22.7 us -> 3.28 us  [the longest x1 3.09 us: shards(): jnp.concatenate([lax.dynamic_slice_in_dim(spread, holder[p], 1, axis=1) f...]
    all_to_all x4 -> x6, starting transfers between devices: 14.9 us -> 26.9 us  [exchange(): return lax.all_to_all(array, axis, split_axis=0, concat_axis=0, tiled=True)]
  transfers between devices with their start and end apart: 9 -> 12, of which waited for: 6 -> 11; matrix products, arithmetic and copies ran while one was open for 9% -> 14% of each run, Pallas kernels for 0% -> 0%
where the time goes in v1:
time: 612 us; the launch traced here: 611 us
  waiting for transfers between devices  428 us (70%)
  local copies, waits for them, and re-layouts  48.9 us (8%)
  starting transfers between devices  37.5 us (6%)
  matrix products  28.2 us (5%)
  blocking collectives  27.8 us (5%)
  between operations  21.5 us (4%)
  other arithmetic  19.1 us (3%)
    all_to_all x6, waiting for transfers between devices, exchange(): return lax.all_to_all(array, axis, split_axis=0, concat_axis=0, tiled=True)  120 us
    reduce_scatter x1, waiting for transfers between devices, forward_by_tokens(): lax.psum_scatter(partial_pre, 'dp', scatter_dimension=0, tiled=True)  111 us
    all_gather x1, waiting for transfers between devices, gradient_by_tokens(): all_scaled = lax.all_gather(flat_scaled, 'dp', axis=0, tiled=True)  81.7 us
    all_to_all x1, waiting for transfers between devices, shards(): lax.all_to_all(ordered.astype(jnp.bfloat16), 'expert', split_axis=1, conc...  58.6 us
    all_gather x1, waiting for transfers between devices, forward_by_tokens(): gathered = lax.all_gather(activation, 'dp', axis=0, tiled=True)  30.6 us
    all_to_all x2, blocking collectives, exchange(): return lax.all_to_all(array, axis, split_axis=0, concat_axis=0, tiled=True)  27.8 us
    all_to_all x6, starting transfers between devices, exchange(): return lax.all_to_all(array, axis, split_axis=0, concat_axis=0, tiled=True)  26.9 us
    unnamed x28, local copies, waits for them, and re-layouts  19.9 us
  transfers between devices with their start and end apart: 12, of which 11 were waited for; matrix products, arithmetic and copies ran while one was open for 14% of the time, Pallas kernels for 0%

profile of v1, /device:TPU:0, one launch (start us, length us, event | category | flops | bytes accessed | tf_op | source)
XLA Modules:
  0.0 610.6 jit_solution(4588306967749927536)
XLA Ops:
  9.1 14.4 %all_to_all.50 = bf16[4,40,2048]{2,1,0:T(8,128)(2,1)} all-to-all(bf16[4,40,2048]{2,1,0:T(8,128)(2,1)S(1)} %bitcast.130), channel_id=1, replica_groups=mesh['dp'=8,'expert'=4] {'expert'}, dimensions={0} | all-to-all | bytes 1310720 | tf_op jit(solution)/shard_map/all_to_all | solution.py:32
  25.1 13.4 %all_to_all.51 = bf16[4,40,2048]{2,1,0:T(8,128)(2,1)} all-to-all(bf16[4,40,2048]{2,1,0:T(8,128)(2,1)S(1)} %bitcast.128), channel_id=1, replica_groups=mesh['dp'=8,'expert'=4] {'expert'}, dimensions={0} | all-to-all | bytes 1310720 | tf_op jit(solution)/shard_map/all_to_all | solution.py:32
  38.4 3.3 copy.52
  43.3 6.2 %all-to-all-start.3 = ((bf16[8,3,144,256]{3,2,1,0:T(8,128)(2,1)}), bf16[8,3,144,256]{3,2,1,0:T(8,128)(2,1)}, u32[]{:S(2)}, u32[]{:S(2)}) async-start(bf16[8,3,144,256]{3,2,1,0:T(8,128)(2,1)} %copy.54), calls=%async_computation.3 | async-start | bytes 3538944 | tf_op jit(solution)/shard_map/all_to_all | solution.py:32
  51.9 68.5 %all-to-all-done.3 = bf16[8,3,144,256]{3,2,1,0:T(8,128)(2,1)} async-done(((bf16[8,3,144,256]{3,2,1,0:T(8,128)(2,1)}), bf16[8,3,144,256]{3,2,1,0:T(8,128)(2,1)}, u32[]{:S(2)}, u32[]{:S(2)}) %all-to-all-start.3) | async-done | bytes 1769504 | tf_op jit(solution)/shard_map/all_to_all | solution.py:32
  120.5 4.2 all-to-all-start
  130.0 8.4 %all-gather.6.cloned.1.call-done = bf16[1280,2048]{1,0:T(8,128)(2,1)} async-done(((bf16[160,2048]{1,0:T(8,128)(2,1)}), bf16[1280,2048]{1,0:T(8,128)(2,1)}) %all-gather.6.cloned.1.call-update) | async-done | bytes 5242896 | tf_op jit(solution)/shard_map/all_gather | solution.py:78
  138.4 5.7 fusion.6
  144.1 81.7 %all-gather.4.cloned.1.call-done = bf16[1280,2048]{1,0:T(8,128)(2,1)} async-done(((bf16[160,2048]{1,0:T(8,128)(2,1)}), bf16[1280,2048]{1,0:T(8,128)(2,1)}) %all-gather.4.cloned.1.call-update) | async-done | bytes 5242896 | tf_op jit(solution)/shard_map/all_gather | solution.py:79
  225.7 5.2 multiply_convert_fusion.3
  237.3 4.3 all-to-all-start.5
  241.6 5.2 copy.53
  246.7 5.2 copy.59
  254.1 28.1 %all-to-all-done.5 = bf16[8,3,144,256]{3,2,1,0:T(8,128)(2,1)} async-done(((bf16[8,3,144,256]{3,2,1,0:T(8,128)(2,1)}), bf16[8,3,144,256]{3,2,1,0:T(8,128)(2,1)}, u32[]{:S(2)}, u32[]{:S(2)}) %all-to-all-start.5) | async-done | bytes 1769504 | tf_op jit(solution)/shard_map/all_to_all | solution.py:32
  282.2 4.2 all-to-all-start.1
  286.6 8.1 %fusion.12 = (bf16[256,3456]{0,1:T(8,128)(2,1)}, bf16[256,3456]{0,1:T(8,128)(2,1)}, bf16[256,3456]{0,1:T(8,128)(2,1)}) fusion(f32[1,256,3456]{1,2,0:T(8,128)} %copy.53, bf16[8,3,144,256]{3,2,1,0:T(8,128)(2,1)} %all-to-all-done.5, f32[1,256,3456]{1,2,0:T(8,128)} %copy.59, f32[1,256,3456]{1,2,0:T(8,128)S(1)} %copy.52), kind=kLoop, calls=%fused_computation.33 | loop fusion | flops 16809984 | bytes 17694720 | tf_op jit(solution)/shard_map/convert.11
  294.7 8.7 %all-to-all-done.1 = bf16[8,160,256]{2,1,0:T(8,128)(2,1)} async-done(((bf16[8,160,256]{2,1,0:T(8,128)(2,1)}), bf16[8,160,256]{2,1,0:T(8,128)(2,1)}, u32[]{:S(2)}, u32[]{:S(2)}) %all-to-all-start.1) | async-done | bytes 655392 | tf_op jit(solution)/shard_map/all_to_all | solution.py:32
  303.4 5.8 fusion
  309.2 110.9 %reduce-scatter.2.cloned.1.call-done = bf16[160,2304]{1,0:T(8,128)(2,1)} async-done(((bf16[1280,2304]{1,0:T(8,128)(2,1)}), bf16[160,2304]{1,0:T(8,128)(2,1)}) %reduce-scatter.2.cloned.1.call-update) | async-done | bytes 737296 | tf_op jit(solution)/shard_map/reduce_scatter | solution.py:140
  424.7 3.8 copy.62
  430.8 3.5 pad_maximum_fusion
  437.1 5.2 all-to-all-start.8
  450.4 30.6 %all-gather.8.cloned.1.call-done = bf16[1280,1152]{1,0:T(8,128)(2,1)} async-done(((bf16[160,1152]{1,0:T(8,128)(2,1)}), bf16[1280,1152]{1,0:T(8,128)(2,1)}) %all-gather.8.cloned.1.call-update) | async-done | bytes 2949136 | tf_op jit(solution)/shard_map/all_gather | solution.py:143
  481.0 3.7 fusion.8
  484.7 17.7 %all-to-all-done.8 = bf16[3,4,64,3456]{3,2,0,1:T(8,128)(2,1)} async-done(((bf16[3,4,64,3456]{3,2,0,1:T(8,128)(2,1)}), bf16[3,4,64,3456]{3,2,0,1:T(8,128)(2,1)}, u32[]{:S(2)}, u32[]{:S(2)}) %all-to-all-start.8) | async-done | bytes 5308448 | tf_op jit(solution)/shard_map/all_to_all | solution.py:214
  502.5 4.5 all-to-all-start.6
  512.9 11.1 %all-to-all-done.6 = bf16[8,160,256]{2,1,0:T(8,128)(2,1)S(1)} async-done(((bf16[8,160,256]{2,1,0:T(8,128)(2,1)}), bf16[8,160,256]{2,1,0:T(8,128)(2,1)S(1)}, u32[]{:S(2)}, u32[]{:S(2)}) %all-to-all-start.6) | async-done | bytes 655392 | tf_op jit(solution)/shard_map/all_to_all | solution.py:32
  524.0 5.1 all-to-all-start.9
  530.7 58.6 %all-to-all-done.9 = bf16[3,4,64,3456]{3,2,0,1:T(8,128)(2,1)} async-done(((bf16[3,4,64,3456]{3,2,0,1:T(8,128)(2,1)}), bf16[3,4,64,3456]{3,2,0,1:T(8,128)(2,1)}, u32[]{:S(2)}, u32[]{:S(2)}) %all-to-all-start.9) | async-done | bytes 5308448 | tf_op jit(solution)/shard_map/all_to_all | solution.py:220
  589.3 3.5 all-to-all-start.7
  592.8 7.0 %fusion.42 = (f32[1,4,64,3456]{3,2,0,1:T(8,128)}, f32[1,4,64,3456]{3,2,0,1:T(8,128)}, f32[1,4,64,3456]{3,2,0,1:T(8,128)}) fusion(bf16[3,4,64,3456]{3,2,0,1:T(8,128)(2,1)} %all-to-all-done.9), kind=kLoop, calls=%fused_computation.87 | loop fusion | bytes 21233664 | tf_op jit(solution)/shard_map/slice | solution.py:240
  599.7 3.2 all-to-all-done.7
  (66 shorter events, 40.3 us)
Async XLA Ops:
  7.2 1.6 copy-start
  7.2 131.2 %all-gather.6.cloned.1.call-start = ((), (), s32[]{:S(2)}) async-start(), calls=%async_computation.12 | async-start | bytes 5898240 | tf_op jit(solution)/shard_map/all_gather | solution.py:78
  23.6 202.2 %all-gather.4.cloned.1.call-start = ((), (), s32[]{:S(2)}) async-start(), calls=%async_computation.11 | async-start | bytes 5898240 | tf_op jit(solution)/shard_map/all_gather | solution.py:79
  41.9 7.6 %copy-start.8 = (s32[128,1]{0,1:T(1,128)S(1)}, s32[128,1]{0,1:T(1,128)}, u32[]{:S(2)}) copy-start(s32[128,1]{0,1:T(1,128)} %param.16) | copy-start | bytes 1540
  43.3 77.2 %all-to-all-start.3 = ((bf16[8,3,144,256]{3,2,1,0:T(8,128)(2,1)}), bf16[8,3,144,256]{3,2,1,0:T(8,128)(2,1)}, u32[]{:S(2)}, u32[]{:S(2)}) async-start(bf16[8,3,144,256]{3,2,1,0:T(8,128)(2,1)} %copy.54), calls=%async_computation.3 | async-start | bytes 3538944 | tf_op jit(solution)/shard_map/all_to_all | solution.py:32
  120.5 116.8 %all-to-all-start = ((bf16[4,40,2048]{2,1,0:T(8,128)(2,1)}), bf16[4,40,2048]{2,1,0:T(8,128)(2,1)}, u32[]{:S(2)}, u32[]{:S(2)}) async-start(bf16[4,40,2048]{2,1,0:T(8,128)(2,1)} %bitcast.124), calls=%async_computation | async-start | bytes 1310720 | tf_op jit(solution)/shard_map/all_to_all | solution.py:32
  225.7 5.2 copy-start.5
  230.9 2.5 copy-start.6
  231.0 2.9 copy-start.9
  237.3 44.9 %all-to-all-start.5 = ((bf16[8,3,144,256]{3,2,1,0:T(8,128)(2,1)}), bf16[8,3,144,256]{3,2,1,0:T(8,128)(2,1)}, u32[]{:S(2)}, u32[]{:S(2)}) async-start(bf16[8,3,144,256]{3,2,1,0:T(8,128)(2,1)} %bitcast.112), calls=%async_computation.5 | async-start | bytes 3538944 | tf_op jit(solution)/shard_map/all_to_all | solution.py:32
  282.2 21.2 %all-to-all-start.1 = ((bf16[8,160,256]{2,1,0:T(8,128)(2,1)}), bf16[8,160,256]{2,1,0:T(8,128)(2,1)}, u32[]{:S(2)}, u32[]{:S(2)}) async-start(bf16[8,160,256]{2,1,0:T(8,128)(2,1)} %copy.51), calls=%async_computation.1 | async-start | bytes 1310720 | tf_op jit(solution)/shard_map/all_to_all | solution.py:32
  286.4 133.8 %reduce-scatter.2.cloned.1.call-start = ((), (), s32[]{:S(2)}) async-start(), calls=%async_computation.13 | async-start | bytes 6635520 | tf_op jit(solution)/shard_map/reduce_scatter | solution.py:140
  309.2 113.2 %copy-start.2 = (bf16[256,3456]{0,1:T(8,128)(2,1)S(1)}, bf16[256,3456]{0,1:T(8,128)(2,1)}, u32[]{:S(2)}) copy-start(bf16[256,3456]{0,1:T(8,128)(2,1)} %get-tuple-element.12) | copy-start | bytes 5308420
  309.2 171.8 %all-gather.8.cloned.1.call-start = ((), (), s32[]{:S(2)}) async-start(), calls=%async_computation.14 | async-start | bytes 3317760 | tf_op jit(solution)/shard_map/all_gather | solution.py:143
  422.4 6.2 %copy-start.3 = (bf16[256,3456]{0,1:T(8,128)(2,1)S(1)}, bf16[256,3456]{0,1:T(8,128)(2,1)}, u32[]{:S(2)}) copy-start(bf16[256,3456]{0,1:T(8,128)(2,1)} %get-tuple-element.13) | copy-start | bytes 5308420
  437.1 5.2 copy-start.7
  437.1 65.4 %all-to-all-start.8 = ((bf16[3,4,64,3456]{3,2,0,1:T(8,128)(2,1)}), bf16[3,4,64,3456]{3,2,0,1:T(8,128)(2,1)}, u32[]{:S(2)}, u32[]{:S(2)}) async-start(bf16[3,4,64,3456]{3,2,0,1:T(8,128)(2,1)} %copy.64), calls=%async_computation.9 | async-start | bytes 10616832 | tf_op jit(solution)/shard_map/all_to_all | solution.py:214
  502.5 21.6 %all-to-all-start.6 = ((bf16[8,160,256]{2,1,0:T(8,128)(2,1)}), bf16[8,160,256]{2,1,0:T(8,128)(2,1)S(1)}, u32[]{:S(2)}, u32[]{:S(2)}) async-start(bf16[8,160,256]{2,1,0:T(8,128)(2,1)} %bitcast.27), calls=%async_computation.7 | async-start | bytes 1310720 | tf_op jit(solution)/shard_map/all_to_all | solution.py:32
  524.0 65.2 %all-to-all-start.9 = ((bf16[3,4,64,3456]{3,2,0,1:T(8,128)(2,1)}), bf16[3,4,64,3456]{3,2,0,1:T(8,128)(2,1)}, u32[]{:S(2)}, u32[]{:S(2)}) async-start(bf16[3,4,64,3456]{3,2,0,1:T(8,128)(2,1)} %pad_maximum_fusion.1), calls=%async_computation.10 | async-start | bytes 10616832 | tf_op jit(solution)/shard_map/all_to_all | solution.py:220
  589.3 13.7 %all-to-all-start.7 = ((bf16[4,40,2048]{2,1,0:T(8,128)(2,1)}), bf16[4,40,2048]{2,1,0:T(8,128)(2,1)S(1)}, u32[]{:S(2)}, u32[]{:S(2)}) async-start(bf16[4,40,2048]{2,1,0:T(8,128)(2,1)} %reshape_reshape.7), calls=%async_computation.8 | async-start | bytes 1310720 | tf_op jit(solution)/shard_map/all_to_all | solution.py:32
  592.7 10.2 %copy-start.4 = (f32[128,1]{0,1:T(1,128)S(1)}, f32[128,1]{0,1:T(1,128)}, u32[]{:S(2)}) copy-start(f32[128,1]{0,1:T(1,128)} %param.17) | copy-start | bytes 1540
  592.8 11.4 %copy-start.1 = (bf16[128,2048]{1,0:T(8,128)(2,1)S(1)}, bf16[128,2048]{1,0:T(8,128)(2,1)}, u32[]{:S(2)}) copy-start(bf16[128,2048]{1,0:T(8,128)(2,1)} %param.11) | copy-start | bytes 1572868
Sparse Core Ops, SparseCore 0:
  23.7 114.7 all-gather.5
  140.6 85.0 all-gather.3
  309.3 110.8 reduce-scatter.1
  422.8 58.1 all-gather.7

commit v2 on v1

--- a/solution.py
+++ b/solution.py
@@ -1,6 +1,7 @@
 import jax
 import jax.numpy as jnp
 from jax import lax
+from jax.experimental.layout import Layout, with_layout_constraint
 from jax.sharding import PartitionSpec as P
 
 D = 2048
@@ -77,7 +78,8 @@
     columns = width // shards_dp
     all_inputs = lax.all_gather(flat_inputs, "dp", axis=0, tiled=True)
     all_scaled = lax.all_gather(flat_scaled, "dp", axis=0, tiled=True)
-    turned = old_weights.astype(jnp.bfloat16).T.reshape(3, shards_dp, columns, depth)
+    rounded = with_layout_constraint(old_weights.astype(jnp.bfloat16), Layout((0, 1)))
+    turned = rounded.T.reshape(3, shards_dp, columns, depth)
     mine = exchange(turned.transpose(1, 0, 2, 3), "dp")
     mine = mine.transpose(1, 2, 0, 3).reshape(3 * columns, shards_dp * depth)
     contract = (((1,), (1,)), ((), ()))
@@ -106,10 +108,10 @@
     grads = jnp.concatenate([gate_up_part.astype(jnp.bfloat16), down_part.astype(jnp.bfloat16)], axis=0)
     grads = grads.reshape(3, columns, shards_dp, depth).transpose(2, 0, 1, 3)
     back = exchange(grads, "dp").transpose(1, 0, 2, 3).reshape(3 * width, depth)
-    return back.T.astype(jnp.float32)
-
-
-def forward_by_weights(flat_rows, new_weights, width, in_scale, out_scale):
+    return with_layout_constraint(back.T, Layout((0, 1))).astype(jnp.float32)
+
+
+def forward_by_weights(flat_rows, new_weights, beside, width, in_scale, out_scale):
     full = lax.all_gather(new_weights, "dp", axis=0, tiled=True)
     gate = jnp.dot(flat_rows, full[:, :width], preferred_element_type=jnp.float32) * in_scale
     up = (
@@ -125,10 +127,10 @@
             preferred_element_type=jnp.float32,
         )
         * out_scale
-    ).astype(jnp.bfloat16)
-
-
-def forward_by_tokens(flat_rows, new_weights, width, in_scale, out_scale):
+    ).astype(jnp.bfloat16), beside
+
+
+def forward_by_tokens(flat_rows, new_weights, beside, width, in_scale, out_scale):
     shards_dp = lax.axis_size("dp")
     depth = new_weights.shape[0]
     count = flat_rows.shape[0]
@@ -140,6 +142,7 @@
     pre = lax.psum_scatter(partial_pre, "dp", scatter_dimension=0, tiled=True).astype(jnp.float32)
     gate, up = pre[:, :width], pre[:, width:]
     activation = (gate * jax.nn.sigmoid(gate) * up).astype(jnp.bfloat16)
+    activation, beside = lax.optimization_barrier((activation, beside))
     gathered = lax.all_gather(activation, "dp", axis=0, tiled=True)
     out = (
         lax.dot_general(
@@ -151,7 +154,7 @@
         * out_scale
     ).astype(jnp.bfloat16)
     back = exchange(out.reshape(shards_dp, count, depth), "dp")
-    return back.transpose(1, 0, 2).reshape(count, shards_dp * depth)
+    return back.transpose(1, 0, 2).reshape(count, shards_dp * depth), beside
 
 
 def dispatch_pairs(targets, payload, capacity):
@@ -208,27 +211,30 @@
     holder = jnp.sum(
         jnp.where(owner_plan[:, None] == positions[None, :], positions[:, None], 0), axis=0
     )
-    stacked = jnp.stack([new_weights, first_new, second_new])
-    rows_here = stacked.shape[1]
-    pieces = stacked.reshape(3, groups, rows_here // groups, stacked.shape[2])
-    spread = lax.all_to_all(
-        pieces.astype(jnp.bfloat16), "expert", split_axis=1, concat_axis=1, tiled=True
-    ).astype(pieces.dtype)
+    rows_here, columns = new_weights.shape
+    pieces = jnp.concatenate(
+        [
+            array.astype(jnp.bfloat16).reshape(groups, 1, rows_here // groups, columns)
+            for array in (new_weights, first_new, second_new)
+        ],
+        axis=1,
+    )
+    spread = exchange(pieces, "expert")
     ordered = jnp.concatenate(
-        [lax.dynamic_slice_in_dim(spread, holder[p], 1, axis=1) for p in range(groups)], axis=1
-    )
-    collected = lax.all_to_all(
-        ordered.astype(jnp.bfloat16), "expert", split_axis=1, concat_axis=1, tiled=True
-    ).astype(ordered.dtype)
-    relocated = collected.reshape(3, rows_here, stacked.shape[2])
+        [lax.dynamic_slice_in_dim(spread, holder[p], 1, axis=0) for p in range(groups)], axis=0
+    )
+    collected = exchange(ordered, "expert")
     next_targets = slot_targets(next_routes, CAP)
     next_pairs = jnp.repeat(next_inputs, topk_count, axis=0)
     send_next = jnp.repeat(dispatch_pairs(next_targets, next_pairs, CAP), split, axis=0)
     received = exchange(send_next, "expert")
     flat_rows = received.reshape(-1, D)
-    partials = (forward_by_tokens if by_tokens else forward_by_weights)(
-        flat_rows, new_weights.astype(jnp.bfloat16), width, in_scale, out_scale
-    )
+    partials, collected = (forward_by_tokens if by_tokens else forward_by_weights)(
+        flat_rows, new_weights.astype(jnp.bfloat16), collected, width, in_scale, out_scale
+    )
+    relocated = [
+        collected[:, at].reshape(1, rows_here, columns).astype(jnp.float32) for at in range(3)
+    ]
     returned = exchange(partials.reshape(received.shape), "expert").reshape(-1, D)
     places = lax.broadcasted_iota(jnp.int32, (next_targets.shape[0], groups * CAP), 1)
     selector = (
@@ -237,7 +243,7 @@
     pair_sums = jnp.dot(selector, returned, preferred_element_type=jnp.float32)
     weighted = pair_sums * next_gates
     layer_output = jnp.sum(weighted.reshape(-1, topk_count, D), axis=1).astype(jnp.bfloat16)
-    return (layer_output, relocated[0][None], relocated[1][None], relocated[2][None])
+    return (layer_output, relocated[0], relocated[1], relocated[2])
 
 
 def solution(mesh):

time: 612 us -> 556 us (0.908)
  waiting for transfers between devices: 428 us -> 391 us
  local copies, waits for them, and re-layouts: 48.9 us -> 24 us
  other arithmetic: 19.1 us -> 29.9 us
    all_to_all x6 -> x8, waiting for transfers between devices: 120 us -> 213 us  [exchange(): return lax.all_to_all(array, axis, split_axis=0, concat_axis=0, tiled=True)]
    reduce_scatter x1, waiting for transfers between devices: 111 us -> 28 us  [forward_by_tokens(): lax.psum_scatter(partial_pre, 'dp', scatter_dimension=0, tiled=True)]
    all_to_all x2 -> x0, waiting for transfers between devices: 76.4 us -> none  [the longest x1 58.6 us: shards(): lax.all_to_all(ordered.astype(jnp.bfloat16), 'expert', split_axis=1, conc...]
    all_gather x1, waiting for transfers between devices: 30.6 us -> 56.7 us  [forward_by_tokens(): gathered = lax.all_gather(activation, 'dp', axis=0, tiled=True)]
    unnamed x28 -> x29, local copies, waits for them, and re-layouts: 19.9 us -> 4.82 us
    convert_element_type x1 -> x4, other arithmetic: 0.17 us -> 14.1 us  [the longest x1 8.03 us: shards(): array.astype(jnp.bfloat16).reshape(groups, 1, rows_here // groups, columns)]
    another operation x4 -> x0, local copies, waits for them, and re-layouts: 11.7 us -> none
    another operation x2 -> x0, other arithmetic: 11.6 us -> none
  transfers between devices with their start and end apart: 12 -> 12, of which waited for: 11 -> 11; matrix products, arithmetic and copies ran while one was open for 14% -> 11% of each run, Pallas kernels for 0% -> 0%
where the time goes in v2:
time: 556 us; the launch traced here: 555 us
  waiting for transfers between devices  391 us (70%)
  starting transfers between devices  34.6 us (6%)
  other arithmetic  29.9 us (5%)
  blocking collectives  27.7 us (5%)
  matrix products  25.7 us (5%)
  local copies, waits for them, and re-layouts  24 us (4%)
  between operations  21.8 us (4%)
    all_to_all x8, waiting for transfers between devices, exchange(): return lax.all_to_all(array, axis, split_axis=0, concat_axis=0, tiled=True)  213 us
    all_gather x1, waiting for transfers between devices, gradient_by_tokens(): all_scaled = lax.all_gather(flat_scaled, 'dp', axis=0, tiled=True)  81.4 us
    all_gather x1, waiting for transfers between devices, forward_by_tokens(): gathered = lax.all_gather(activation, 'dp', axis=0, tiled=True)  56.7 us
    all_to_all x8, starting transfers between devices, exchange(): return lax.all_to_all(array, axis, split_axis=0, concat_axis=0, tiled=True)  34.3 us
    reduce_scatter x1, waiting for transfers between devices, forward_by_tokens(): lax.psum_scatter(partial_pre, 'dp', scatter_dimension=0, tiled=True)  28 us
    all_to_all x2, blocking collectives, exchange(): return lax.all_to_all(array, axis, split_axis=0, concat_axis=0, tiled=True)  27.7 us
    all_gather x1, waiting for transfers between devices, gradient_by_tokens(): all_inputs = lax.all_gather(flat_inputs, 'dp', axis=0, tiled=True)  12.1 us
  transfers between devices with their start and end apart: 12, of which 11 were waited for; matrix products, arithmetic and copies ran while one was open for 11% of the time, Pallas kernels for 0%

profile of v2, /device:TPU:0, one launch (start us, length us, event | category | flops | bytes accessed | tf_op | source)
XLA Modules:
  0.0 554.9 jit_solution(12143461922377390193)
XLA Ops:
  9.2 14.4 %all_to_all.50 = bf16[4,40,2048]{2,1,0:T(8,128)(2,1)} all-to-all(bf16[4,40,2048]{2,1,0:T(8,128)(2,1)S(1)} %bitcast.135), channel_id=1, replica_groups=mesh['dp'=8,'expert'=4] {'expert'}, dimensions={0} | all-to-all | bytes 1310720 | tf_op jit(solution)/shard_map/all_to_all | solution.py:33
  24.1 13.4 %all_to_all.51 = bf16[4,40,2048]{2,1,0:T(8,128)(2,1)} all-to-all(bf16[4,40,2048]{2,1,0:T(8,128)(2,1)S(1)} %bitcast.133), channel_id=1, replica_groups=mesh['dp'=8,'expert'=4] {'expert'}, dimensions={0} | all-to-all | bytes 1310720 | tf_op jit(solution)/shard_map/all_to_all | solution.py:33
  37.5 3.4 fusion.14
  40.9 2.6 copy.42
  44.8 6.4 %all-to-all-start.3 = ((bf16[8,3,144,256]{3,2,1,0:T(8,128)(2,1)}), bf16[8,3,144,256]{3,2,1,0:T(8,128)(2,1)S(1)}, u32[]{:S(2)}, u32[]{:S(2)}) async-start(bf16[8,3,144,256]{3,2,1,0:T(8,128)(2,1)} %copy.43), calls=%async_computation.3 | async-start | bytes 3538944 | tf_op jit(solution)/shard_map/all_to_all | solution.py:33
  52.5 68.3 %all-to-all-done.3 = bf16[8,3,144,256]{3,2,1,0:T(8,128)(2,1)S(1)} async-done(((bf16[8,3,144,256]{3,2,1,0:T(8,128)(2,1)}), bf16[8,3,144,256]{3,2,1,0:T(8,128)(2,1)S(1)}, u32[]{:S(2)}, u32[]{:S(2)}) %all-to-all-start.3) | async-done | bytes 1769504 | tf_op jit(solution)/shard_map/all_to_all | solution.py:33
  120.9 3.5 all-to-all-start
  126.6 12.1 %all-gather.6.cloned.1.call-done = bf16[1280,2048]{1,0:T(8,128)(2,1)} async-done(((bf16[160,2048]{1,0:T(8,128)(2,1)}), bf16[1280,2048]{1,0:T(8,128)(2,1)}) %all-gather.6.cloned.1.call-update) | async-done | bytes 5242896 | tf_op jit(solution)/shard_map/all_gather | solution.py:79
  138.7 5.7 %fusion.6 = f32[288,1280]{1,0:T(8,128)} fusion(bf16[1280,2048]{1,0:T(8,128)(2,1)} %all-gather.6.cloned.1.call-done, bf16[288,2048]{1,0:T(8,128)(2,1)} %bitcast.136), kind=kOutput, calls=%fused_computation.16 | convolution fusion | flops 1510318080 | bytes 7897088 | tf_op jit(solution)/shard_map/dot_general | solution.py:87
  144.3 81.4 %all-gather.4.cloned.1.call-done = bf16[1280,2048]{1,0:T(8,128)(2,1)} async-done(((bf16[160,2048]{1,0:T(8,128)(2,1)}), bf16[1280,2048]{1,0:T(8,128)(2,1)}) %all-gather.4.cloned.1.call-update) | async-done | bytes 5242896 | tf_op jit(solution)/shard_map/all_gather | solution.py:80
  225.8 5.0 multiply_convert_fusion.3
  237.1 3.6 all-to-all-start.5
  241.8 39.4 %all-to-all-done.5 = bf16[8,3,144,256]{3,2,1,0:T(8,128)(2,1)S(1)} async-done(((bf16[8,3,144,256]{3,2,1,0:T(8,128)(2,1)}), bf16[8,3,144,256]{3,2,1,0:T(8,128)(2,1)S(1)}, u32[]{:S(2)}, u32[]{:S(2)}) %all-to-all-start.5) | async-done | bytes 1769504 | tf_op jit(solution)/shard_map/all_to_all | solution.py:33
  281.2 3.6 all-to-all-start.1
  286.4 2.7 copy.48
  289.2 8.0 %fusion.12 = (bf16[256,3456]{1,0:T(8,128)(2,1)}, bf16[256,3456]{1,0:T(8,128)(2,1)}, bf16[256,3456]{1,0:T(8,128)(2,1)}) fusion(f32[1,256,3456]{2,1,0:T(8,128)} %param.19, bf16[3456,256]{0,1:T(8,128)(2,1)S(1)} %copy.48, f32[1,256,3456]{2,1,0:T(8,128)} %param.20, f32[1,256,3456]{2,1,0:T(8,128)} %param.18), kind=kLoop, calls=%fused_computation.29 | loop fusion | flops 16809984 | bytes 17694720 | tf_op jit(solution)/shard_map/convert_element_type | solution.py:217
  297.2 5.1 all-to-all-done.1
  302.3 5.5 fusion
  309.3 5.1 pad_maximum_fusion
  314.5 5.2 all-to-all-start.6
  328.1 51.7 %all-to-all-done.6 = bf16[4,3,64,3456]{3,2,1,0:T(8,128)(2,1)} async-done(((bf16[4,3,64,3456]{3,2,1,0:T(8,128)(2,1)}), bf16[4,3,64,3456]{3,2,1,0:T(8,128)(2,1)}, u32[]{:S(2)}, u32[]{:S(2)}) %all-to-all-start.6) | async-done | bytes 5308448 | tf_op jit(solution)/shard_map/all_to_all | solution.py:33
  379.8 2.9 constant_dynamic-slice_fusion.2
  382.7 3.0 pad_maximum_fusion.1
  385.8 5.1 all-to-all-start.7
  390.9 28.0 %reduce-scatter.2.cloned.1.call-done = bf16[160,2304]{1,0:T(8,128)(2,1)} async-done(((bf16[1280,2304]{1,0:T(8,128)(2,1)}), bf16[160,2304]{1,0:T(8,128)(2,1)}) %reduce-scatter.2.cloned.1.call-update) | async-done | bytes 737296 | tf_op jit(solution)/shard_map/reduce_scatter | solution.py:142
  421.0 30.0 %all-to-all-done.7 = bf16[4,3,64,3456]{3,2,1,0:T(8,128)(2,1)} async-done(((bf16[4,3,64,3456]{3,2,1,0:T(8,128)(2,1)}), bf16[4,3,64,3456]{3,2,1,0:T(8,128)(2,1)}, u32[]{:S(2)}, u32[]{:S(2)}) %all-to-all-start.7) | async-done | bytes 5308448 | tf_op jit(solution)/shard_map/all_to_all | solution.py:33
  451.0 56.7 %all-gather.8.cloned.1.call-done = bf16[1280,1152]{1,0:T(8,128)(2,1)} async-done(((bf16[160,1152]{1,0:T(8,128)(2,1)}), bf16[1280,1152]{1,0:T(8,128)(2,1)}) %all-gather.8.cloned.1.call-update) | async-done | bytes 2949136 | tf_op jit(solution)/shard_map/all_gather | solution.py:146
  507.7 3.7 fusion.8
  511.4 3.5 all-to-all-start.8
  515.0 17.0 %all-to-all-done.8 = bf16[8,160,256]{2,1,0:T(8,128)(2,1)S(1)} async-done(((bf16[8,160,256]{2,1,0:T(8,128)(2,1)}), bf16[8,160,256]{2,1,0:T(8,128)(2,1)S(1)}, u32[]{:S(2)}, u32[]{:S(2)}) %all-to-all-start.8) | async-done | bytes 655392 | tf_op jit(solution)/shard_map/all_to_all | solution.py:33
  533.5 3.5 all-to-all-start.9
  537.0 2.9 fusion.43
  (69 shorter events, 30.6 us)
Async XLA Ops:
  7.2 1.7 copy-start
  7.2 16.5 %copy-start.5 = (f32[128,1]{0,1:T(1,128)S(1)}, f32[128,1]{0,1:T(1,128)}, u32[]{:S(2)}) copy-start(f32[128,1]{0,1:T(1,128)} %param.14) | copy-start | bytes 1540
  7.2 16.5 %copy-start.4 = (bf16[128,2048]{1,0:T(8,128)(2,1)S(1)}, bf16[128,2048]{1,0:T(8,128)(2,1)}, u32[]{:S(2)}) copy-start(bf16[128,2048]{1,0:T(8,128)(2,1)} %param.12) | copy-start | bytes 1572868
  7.2 131.5 %all-gather.6.cloned.1.call-start = ((), (), s32[]{:S(2)}) async-start(), calls=%async_computation.12 | async-start | bytes 5898240 | tf_op jit(solution)/shard_map/all_gather | solution.py:79
  23.6 202.2 %all-gather.4.cloned.1.call-start = ((), (), s32[]{:S(2)}) async-start(), calls=%async_computation.11 | async-start | bytes 5898240 | tf_op jit(solution)/shard_map/all_gather | solution.py:80
  44.8 6.4 %copy-start.10 = (s32[128,1]{0,1:T(1,128)S(1)}, s32[128,1]{0,1:T(1,128)}, u32[]{:S(2)}) copy-start(s32[128,1]{0,1:T(1,128)} %param.16) | copy-start | bytes 1540
  44.8 6.5 %copy-start.3 = (bf16[128,2048]{1,0:T(8,128)(2,1)S(1)}, bf16[128,2048]{1,0:T(8,128)(2,1)}, u32[]{:S(2)}) copy-start(bf16[128,2048]{1,0:T(8,128)(2,1)} %param.15) | copy-start | bytes 1572868
  44.8 76.0 %all-to-all-start.3 = ((bf16[8,3,144,256]{3,2,1,0:T(8,128)(2,1)}), bf16[8,3,144,256]{3,2,1,0:T(8,128)(2,1)S(1)}, u32[]{:S(2)}, u32[]{:S(2)}) async-start(bf16[8,3,144,256]{3,2,1,0:T(8,128)(2,1)} %copy.43), calls=%async_computation.3 | async-start | bytes 3538944 | tf_op jit(solution)/shard_map/all_to_all | solution.py:33
  120.9 116.2 %all-to-all-start = ((bf16[4,40,2048]{2,1,0:T(8,128)(2,1)}), bf16[4,40,2048]{2,1,0:T(8,128)(2,1)S(1)}, u32[]{:S(2)}, u32[]{:S(2)}) async-start(bf16[4,40,2048]{2,1,0:T(8,128)(2,1)} %bitcast.129), calls=%async_computation | async-start | bytes 1310720 | tf_op jit(solution)/shard_map/all_to_all | solution.py:33
  225.8 5.0 copy-start.7
  230.8 2.5 copy-start.8
  230.8 2.9 copy-start.11
  237.1 44.2 %all-to-all-start.5 = ((bf16[8,3,144,256]{3,2,1,0:T(8,128)(2,1)}), bf16[8,3,144,256]{3,2,1,0:T(8,128)(2,1)S(1)}, u32[]{:S(2)}, u32[]{:S(2)}) async-start(bf16[8,3,144,256]{3,2,1,0:T(8,128)(2,1)} %bitcast.118), calls=%async_computation.5 | async-start | bytes 3538944 | tf_op jit(solution)/shard_map/all_to_all | solution.py:33
  281.2 21.1 %all-to-all-start.1 = ((bf16[8,160,256]{2,1,0:T(8,128)(2,1)}), bf16[8,160,256]{2,1,0:T(8,128)(2,1)S(1)}, u32[]{:S(2)}, u32[]{:S(2)}) async-start(bf16[8,160,256]{2,1,0:T(8,128)(2,1)} %copy.41), calls=%async_computation.1 | async-start | bytes 1310720 | tf_op jit(solution)/shard_map/all_to_all | solution.py:33
  284.9 134.0 %reduce-scatter.2.cloned.1.call-start = ((), (), s32[]{:S(2)}) async-start(), calls=%async_computation.13 | async-start | bytes 6635520 | tf_op jit(solution)/shard_map/reduce_scatter | solution.py:142
  307.9 1.5 copy-start.2
  314.5 5.2 copy-start.9
  314.5 65.4 %all-to-all-start.6 = ((bf16[4,3,64,3456]{3,2,1,0:T(8,128)(2,1)}), bf16[4,3,64,3456]{3,2,1,0:T(8,128)(2,1)}, u32[]{:S(2)}, u32[]{:S(2)}) async-start(bf16[4,3,64,3456]{3,2,1,0:T(8,128)(2,1)} %pad_maximum_fusion), calls=%async_computation.7 | async-start | bytes 10616832 | tf_op jit(solution)/shard_map/all_to_all | solution.py:33
  385.8 65.2 %all-to-all-start.7 = ((bf16[4,3,64,3456]{3,2,1,0:T(8,128)(2,1)}), bf16[4,3,64,3456]{3,2,1,0:T(8,128)(2,1)}, u32[]{:S(2)}, u32[]{:S(2)}) async-start(bf16[4,3,64,3456]{3,2,1,0:T(8,128)(2,1)} %pad_maximum_fusion.1), calls=%async_computation.8 | async-start | bytes 10616832 | tf_op jit(solution)/shard_map/all_to_all | solution.py:33
  390.8 116.9 %all-gather.8.cloned.1.call-start = ((), (), s32[]{:S(2)}) async-start(), calls=%async_computation.14 | async-start | bytes 3317760 | tf_op jit(solution)/shard_map/all_gather | solution.py:146
  511.4 20.6 %all-to-all-start.8 = ((bf16[8,160,256]{2,1,0:T(8,128)(2,1)}), bf16[8,160,256]{2,1,0:T(8,128)(2,1)S(1)}, u32[]{:S(2)}, u32[]{:S(2)}) async-start(bf16[8,160,256]{2,1,0:T(8,128)(2,1)} %bitcast.35), calls=%async_computation.9 | async-start | bytes 1310720 | tf_op jit(solution)/shard_map/all_to_all | solution.py:33
  533.5 13.7 %all-to-all-start.9 = ((bf16[4,40,2048]{2,1,0:T(8,128)(2,1)}), bf16[4,40,2048]{2,1,0:T(8,128)(2,1)S(1)}, u32[]{:S(2)}, u32[]{:S(2)}) async-start(bf16[4,40,2048]{2,1,0:T(8,128)(2,1)} %reshape_reshape.7), calls=%async_computation.10 | async-start | bytes 1310720 | tf_op jit(solution)/shard_map/all_to_all | solution.py:33
  544.0 4.4 copy-start.1
  544.0 3.3 copy-start.6
Sparse Core Ops, SparseCore 0:
  23.7 114.9 all-gather.5
  140.9 84.8 all-gather.3
  308.0 110.8 reduce-scatter.1
  451.1 56.5 all-gather.7
